TPU v7x, 256 devices: a whole 4x4x8 slice. The times are simulated.
256 devices in a mesh: pt: 32 (over z, x), lm: 8 (over y, core).
Axes of the slice: x: 4, y: 4, z: 8, core: 2. Of those that a mesh axis runs over, the one named last changes fastest.
Arguments:
- points: float32 [262144, 256], P('pt'), may hold values from -6 to 6
- landmarks: float32 [8192, 256], P(('lm', 'pt')), may hold values from -6 to 6
- block_vec: float32 [8192, 32], P(('lm', 'pt')), may hold values from -6 to 6
Outputs:
- new_block: float32 [8192, 32], P(('lm', 'pt'))
- projected: float32 [262144, 32], P('pt')
All inputs are finite; a program needn't handle non-finite values.
Results may differ from a plain program's by a relative error of at most 0.0056.
Values may be sent and summed in bfloat16 or wider, within the bound.
A program may use at most 128 MiB of HBM per device.

v0:
```python
import math

import jax
import jax.numpy as jnp
from jax import lax
from jax.sharding import PartitionSpec as P


def normalize(rows):
    return (rows * lax.rsqrt(jnp.sum(rows * rows, axis=1, keepdims=True) + 1e-06)).astype(
        jnp.bfloat16
    )


def on_device(points, landmarks, block_vec):
    unit_pts = normalize(points)
    unit_lms = normalize(landmarks)
    count = unit_pts.shape[0]
    stride = 1024
    pieces_pts = unit_pts.reshape(count // stride, stride, unit_pts.shape[1])
    vectors = lax.all_gather(block_vec, "pt", axis=0, tiled=True)
    width = vectors.shape[0]
    total_points = count * lax.axis_size("pt")
    total_landmarks = width * lax.axis_size("lm")
    piece = lax.all_gather(unit_lms, "pt", axis=0, tiled=True)

    def one(rows):
        scores = lax.dot_general(
            rows, piece, (((1,), (1,)), ((), ())), preferred_element_type=jnp.float32
        )
        return jnp.exp(16.0 * scores).astype(jnp.bfloat16)

    tile = lax.map(one, pieces_pts).reshape(count, piece.shape[0])
    row_part = jnp.sum(tile, axis=1, dtype=jnp.float32)
    col_part = jnp.sum(tile, axis=0, dtype=jnp.float32)
    col_mean = lax.psum(col_part, "pt") / total_points
    row_sum = lax.psum(row_part, "lm")
    scaled = (vectors * lax.rsqrt(col_mean)[:, None]).astype(jnp.bfloat16)
    product_part = jnp.dot(tile, scaled, preferred_element_type=jnp.float32)
    product_sum = lax.psum(product_part, "lm")
    row_scale = lax.rsqrt(row_sum / total_landmarks)[:, None]
    projected = product_sum * row_scale * (1.0 / math.sqrt(total_landmarks))
    carried = (projected * row_scale).astype(jnp.bfloat16)
    back_part = lax.dot_general(
        tile, carried, (((0,), (0,)), ((), ())), preferred_element_type=jnp.float32
    )
    own_back = lax.psum_scatter(back_part, "pt", scatter_dimension=0, tiled=True)
    owned = own_back.shape[0]
    own_mean = lax.dynamic_slice_in_dim(col_mean, lax.axis_index("pt") * owned, owned, 0)
    new_block = own_back * lax.rsqrt(own_mean)[:, None] * (1.0 / math.sqrt(total_points))
    return (new_block, projected)


def solution(mesh):
    return jax.shard_map(
        on_device,
        mesh=mesh,
        in_specs=(P("pt", None), P(("lm", "pt"), None), P(("lm", "pt"), None)),
        out_specs=(P(("lm", "pt"), None), P("pt", None)),
        check_vma=False,
    )
```

profile of v0, /device:TPU:1, one launch (start us, length us, event | category | flops | bytes accessed | tf_op | source)
XLA Modules:
  0.0 528.0 jit_solution(5405454407708766737)
XLA Ops:
  7.2 0.0 copy-start.1
  7.2 0.0 all-reduce.2.cloned.1.call-start
  7.2 4.5 multiply_reduce_fusion
  11.8 5.4 %multiply_convert_fusion = bf16[8192,256]{1,0:T(8,128)(2,1)} fusion(f32[8192,256]{1,0:T(8,128)} %param.5, f32[8192]{0:T(1024)S(1)} %add_rsqrt_fusion), kind=kLoop, calls=%fused_computation.7 | loop fusion | flops 4194304 | bytes 12615680 | tf_op jit(solution)/shard_map/convert_element_type | solution.py:10
  17.2 0.0 copy-done.1
  17.2 0.1 multiply_reduce_fusion.1
  17.3 0.1 multiply_convert_fusion.5
  17.4 41.4 %all_gather.6 = bf16[1024,256]{1,0:T(8,128)(2,1)S(1)} all-gather(bf16[32,256]{1,0:T(8,128)(2,1)S(1)} %multiply_convert_fusion.5), channel_id=1, replica_groups=mesh['pt'=32,'lm'=8] {'pt'}, dimensions={0}, use_global_device_ids=true | all-gather | bytes 540672 | tf_op jit(solution)/shard_map/all_gather | solution.py:25
  58.8 0.0 copy-start.2
  58.8 25.0 %while.10 = (s32[]{:T(128)}, bf16[8,1024,1024]{2,1,0:T(8,128)(2,1)}, bf16[8,1024,256]{2,1,0:T(8,128)(2,1)}, bf16[1024,256]{1,0:T(8,128)(2,1)S(1)}, s32[]{:T(128)}) while((s32[]{:T(128)}, bf16[8,1024,1024]{2,1,0:T(8,128)(2,1)}, bf16[8,1024,256]{2,1,0:T(8,128)(2,1)}, bf16[1024,256]{1,0:T(8,128)(2,1)S(1)}, s32[]{:T(128)}) %tuple.32), condition=%wide.region_3.4_spmd, body=%wide.region_2.3_spmd.sunk | while | flops 538968064 | bytes 3146813 | solution.py:33
  58.8 3.2 bitcast_dynamic-update-slice_fusion.2
  61.9 3.1 bitcast_dynamic-update-slice_fusion.2
  65.0 3.1 bitcast_dynamic-update-slice_fusion.2
  68.1 3.1 bitcast_dynamic-update-slice_fusion.2
  71.3 3.2 bitcast_dynamic-update-slice_fusion.2
  74.5 3.1 bitcast_dynamic-update-slice_fusion.2
  77.5 3.1 bitcast_dynamic-update-slice_fusion.2
  80.7 3.1 bitcast_dynamic-update-slice_fusion.2
  83.8 8.0 %convert_reduce_fusion = (f32[8,1024]{1,0:T(8,128)S(1)}, f32[1024]{0:T(1024)S(1)}) fusion(bf16[8,1024,1024]{2,1,0:T(8,128)(2,1)} %get-tuple-element.24), kind=kLoop, calls=%fused_computation.5 | loop fusion | flops 25156608 | bytes 16814080 | tf_op jit(solution)/shard_map/reduce_sum | solution.py:34
  91.8 58.1 %psum.21 = f32[1024]{0:T(1024)S(1)} all-reduce(f32[1024]{0:T(1024)S(1)} %get-tuple-element.26), channel_id=1, replica_groups=mesh['pt'=32,'lm'=8] {'pt'}, use_global_device_ids=true, to_apply=%region_5.6 | all-reduce | flops 1024 | bytes 8192 | tf_op jit(solution)/shard_map/psum | solution.py:36
  149.9 0.0 copy-done.2
  149.9 34.2 %all_gather.7 = f32[1024,32]{1,0:T(8,128)S(1)} all-gather(f32[32,32]{1,0:T(8,128)S(1)} %copy-done.2), channel_id=1, replica_groups=mesh['pt'=32,'lm'=8] {'pt'}, dimensions={0}, use_global_device_ids=true | all-gather | bytes 135168 | tf_op jit(solution)/shard_map/all_gather | solution.py:21
  184.1 11.8 %fusion.6 = f32[8192,32]{0,1:T(8,128)} fusion(bf16[8192,1024]{1,0:T(8,128)(2,1)} %bitcast.20, f32[1024,32]{1,0:T(8,128)S(1)} %all_gather.7, f32[1024]{0:T(1024)S(1)} %get-tuple-element.38), kind=kOutput, calls=%fused_computation.15 | convolution fusion | flops 536936448 | bytes 17960960 | tf_op jit(solution)/shard_map/dot_general | solution.py:39
  195.9 0.0 all-reduce.2.cloned.1.call-update
  196.0 0.0 reduce-scatter.2.cloned.1.call-start
  196.0 59.0 %psum.23 = f32[8192]{0:T(1024)S(1)} all-reduce(f32[8192]{0:T(1024)S(1)} %bitcast.24), channel_id=1, replica_groups=mesh['pt'=32,'lm'=8] {'lm'}, use_global_device_ids=true, to_apply=%region_8.9 | all-reduce | flops 8192 | bytes 65536 | tf_op jit(solution)/shard_map/psum | solution.py:37
  255.1 0.1 dynamic-slice_rsqrt_fusion
  255.2 44.2 %all-reduce.2.cloned.1.call-done = f32[8192,32]{0,1:T(8,128)} async-done(((f32[8192,32]{0,1:T(8,128)}), f32[8192,32]{0,1:T(8,128)}) %all-reduce.2.cloned.1.call-update) | async-done | bytes 1048592 | tf_op jit(solution)/shard_map/psum | solution.py:40
  299.4 0.0 copy-start
  299.4 11.4 %fusion.3 = f32[1024,32]{1,0:T(8,128)} fusion(bf16[8192,1024]{1,0:T(8,128)(2,1)} %bitcast.21, f32[8192,32]{0,1:T(8,128)} %all-reduce.2.cloned.1.call-done, f32[8192]{0:T(1024)S(1)} %get-tuple-element.36, f32[8192]{0:T(1024)S(1)} %get-tuple-element.35), kind=kOutput, calls=%fused_computation.11 | convolution fusion | flops 537657344 | bytes 18022400 | tf_op jit(solution)/shard_map/dot_general | solution.py:44
  310.8 0.0 reduce-scatter.2.cloned.1.call-update
  310.8 0.0 copy-done
  310.8 1.1 multiply_multiply_fusion
  311.9 207.9 %reduce-scatter.2.cloned.1.call-done = f32[32,32]{1,0:T(8,128)} async-done(((f32[1024,32]{1,0:T(8,128)}), f32[32,32]{1,0:T(8,128)}) %reduce-scatter.2.cloned.1.call-update) | async-done | bytes 4112 | tf_op jit(solution)/shard_map/reduce_scatter | solution.py:47
  519.8 1.4 multiply_multiply_fusion.1
  (6 shorter events, 0.0 us)
Async XLA Ops:
  7.2 10.0 %copy-start.1 = (f32[32,256]{1,0:T(8,128)S(1)}, f32[32,256]{1,0:T(8,128)}, u32[]{:S(2)}) copy-start(f32[32,256]{1,0:T(8,128)} %param.6) | copy-start | bytes 98308
  7.2 292.2 %all-reduce.2.cloned.1.call-start = ((), (), s32[]{:S(2)}) async-start(), calls=%async_computation.1 | async-start | bytes 2097152 | tf_op jit(solution)/shard_map/psum | solution.py:40
  58.8 91.1 %copy-start.2 = (f32[32,32]{1,0:T(8,128)S(1)}, f32[32,32]{1,0:T(8,128)}, u32[]{:S(2)}) copy-start(f32[32,32]{1,0:T(8,128)} %param.7) | copy-start | bytes 12292
  196.0 323.8 %reduce-scatter.2.cloned.1.call-start = ((), (), s32[]{:S(2)}) async-start(), calls=%async_computation.2 | async-start | bytes 540672 | tf_op jit(solution)/shard_map/reduce_scatter | solution.py:47
  299.4 11.4 %copy-start = (f32[8192,32]{0,1:T(8,128)S(1)}, f32[8192,32]{0,1:T(8,128)}, u32[]{:S(2)}) copy-start(f32[8192,32]{0,1:T(8,128)} %all-reduce.2.cloned.1.call-done) | copy-start | bytes 3145732
Sparse Core Ops, SparseCore 0:
  196.1 103.2 all-reduce.1
  310.9 208.7 reduce-scatter.1
where the time goes:
time: 533 us; the launch traced here: 528 us
  waiting for transfers between devices  252 us (47%)
  blocking collectives  193 us (36%)
  matrix products  48.3 us (9%)
  other arithmetic  20.6 us (4%)
  between operations  14.1 us (3%)
    reduce_scatter x1, waiting for transfers between devices, on_device(): lax.psum_scatter(back_part, 'pt', scatter_dimension=0, tiled=True)  208 us
    psum x1, blocking collectives, on_device(): row_sum = lax.psum(row_part, 'lm')  59 us
    psum x1, blocking collectives, on_device(): col_mean = lax.psum(col_part, 'pt') / total_points  58.1 us
    psum x1, waiting for transfers between devices, on_device(): product_sum = lax.psum(product_part, 'lm')  44.2 us
    all_gather x1, blocking collectives, on_device(): piece = lax.all_gather(unit_lms, 'pt', axis=0, tiled=True)  41.4 us
    all_gather x1, blocking collectives, on_device(): vectors = lax.all_gather(block_vec, 'pt', axis=0, tiled=True)  34.2 us
    dot_general x8, matrix products, one(): lax.dot_general(rows, piece, (((1,), (1,)), ((), ())), preferred_element_...  25 us
    dot_general x1, matrix products, on_device(): product_part = jnp.dot(tile, scaled, preferred_element_type=jnp.float32)  11.8 us
  transfers between devices with their start and end apart: 2, of which 2 were waited for; matrix products, arithmetic and copies ran while one was open for 0% of the time, Pallas kernels for 0%

commit v1 on v0

v1 whole, which is shorter than its diff:
```python
import functools
import math

import jax
import jax.numpy as jnp
from jax import lax
from jax.experimental import pallas as pl
from jax.experimental.pallas import tpu as pltpu
from jax.sharding import PartitionSpec as P

MESH = pl.DeviceIdType.MESH
NX = 4
PAIR = 256
EXP2_SCALE = 16.0 / math.log(2.0)
LAST = (((1,), (1,)), ((), ()))


def unit_rows(rows):
    return (rows * lax.rsqrt(jnp.sum(rows * rows, axis=1, keepdims=True) + 1e-06)).astype(
        jnp.bfloat16
    )


def at(start, size):
    return pl.ds(pl.multiple_of(start, size), size)


def kernel(
    npt, nlm, total_points, total_landmarks,
    points, landmarks, vectors, new_block, projected,
    raw, unit, lms, tile, tile_t, cols_x, cols_z, col_inv, vec_x, vec_z, scaled, rows_all, rows_inv,
    part, part_in, proj, back_out, back_in, back_x,
    raw_sem, lz_s, lz_r, lx_s, lx_r, vx_s, vx_r, vz_s, vz_r, cx_s, cx_r, cz_s, cz_r,
    row_s, row_r, ps_s, ps_r, pg_s, pg_r, bz_s, bz_r, bx_s, bx_r,
):
    count, depth = unit.shape
    own, width = vectors.shape
    nz = npt // NX
    group = NX * own
    chunks = part_in.shape[0]
    chunk = count // chunks
    piece = chunk // nlm
    pt = lax.axis_index("pt")
    lm = lax.axis_index("lm")
    z, x = pt // NX, lax.rem(pt, NX)

    def z_at(step):
        return lax.rem(z + step, nz)

    def x_at(step):
        return lax.rem(x + step, NX)

    def lm_at(step):
        return lax.rem(lm + step, nlm)

    def z_dev(step):
        return (z_at(step) * NX + x, lm)

    def x_dev(step):
        return (z * NX + x_at(step), lm)

    def lm_dev(step):
        return (pt, lm_at(step))

    def remote(src, dst, send, recv, device):
        return pltpu.make_async_remote_copy(
            src_ref=src, dst_ref=dst, send_sem=send, recv_sem=recv,
            device_id=device, device_id_type=MESH,
        )

    sent = []

    def send(*args):
        copy = remote(*args)
        copy.start()
        sent.append(copy)
        return copy

    z_order = [1, nz - 1, 2, nz - 2, 3, nz - 3, 4]
    x_order = [1, 3, 2]
    lm_order = list(range(1, nlm))

    parts = raw_sem.shape[0]
    rows_in = count // parts
    loads = [
        pltpu.make_async_copy(
            points.at[pl.ds(i * rows_in, rows_in), :],
            raw.at[pl.ds(i * rows_in, rows_in), :],
            raw_sem.at[i],
        )
        for i in range(parts)
    ]
    for load in loads:
        load.start()

    barrier = pltpu.get_barrier_semaphore()
    for d in z_order:
        pl.semaphore_signal(barrier, inc=1, device_id=z_dev(d), device_id_type=MESH)
    for e in x_order:
        pl.semaphore_signal(barrier, inc=1, device_id=x_dev(e), device_id_type=MESH)
    for f in lm_order:
        pl.semaphore_signal(barrier, inc=1, device_id=lm_dev(f), device_id_type=MESH)

    lms[at(pt * own, own), :] = unit_rows(landmarks[...])
    lane = lax.broadcasted_iota(jnp.int32, (width, group), 1)
    wide = jnp.concatenate([vectors[...], jnp.zeros((own, group - width), jnp.float32)], axis=1)
    turned = jnp.concatenate([wide] * NX, axis=0).T[:width, :]
    vec_x[x] = jnp.where(lane // own == x, turned, 0.0)

    pl.semaphore_wait(barrier, len(z_order) + len(x_order) + len(lm_order))

    def lm_rows(zz, xx):
        return lms.at[at((zz * NX + xx) * own, own), :]

    mine = lm_rows(z, x)
    for d in z_order:
        send(mine, mine, lz_s.at[d], lz_r.at[d], z_dev(d))
    for e in x_order:
        send(mine, mine, lx_s.at[e], lx_r.at[e], x_dev(e))
    vec_copies = [send(vec_x.at[x], vec_x.at[x], vx_s.at[e], vx_r.at[e], x_dev(e)) for e in x_order]

    for i, load in enumerate(loads):
        load.wait()
        rows = pl.ds(i * rows_in, rows_in)
        unit[rows, :] = unit_rows(raw[rows, :])

    for d in z_order:
        block = lm_rows(z_at(nz - d), x)
        remote(block, block, lz_s.at[d], lz_r.at[d], z_dev(d)).wait_recv()
        for e in x_order:
            send(block, block, lx_s.at[d * NX + e], lx_r.at[d * NX + e], x_dev(e))
    for copy in vec_copies:
        copy.wait_recv()
    vec_z[z] = jnp.sum(vec_x[...], axis=0)
    vec_copies = [send(vec_z.at[z], vec_z.at[z], vz_s.at[d], vz_r.at[d], z_dev(d)) for d in z_order]

    def pair(j, _):
        steps = (lax.rem(nz - j, nz), j + 1)
        groups = [z_at(nz - step) for step in steps]
        for step in steps:
            for e in x_order:
                sem = step * NX + e
                remote(mine, mine, lx_s.at[sem], lx_r.at[sem], x_dev(e)).wait_recv()
        weights = jnp.concatenate([lms[at(g * group, group), :] for g in groups], axis=0)
        scores = lax.dot_general(unit[...], weights, LAST, preferred_element_type=jnp.float32)
        values = jnp.exp2(EXP2_SCALE * scores)
        rounded = values.astype(jnp.bfloat16)
        sums = jnp.sum(values, axis=0, keepdims=True)
        for i, g in enumerate(groups):
            lanes = slice(i * group, (i + 1) * group)
            tile[:, at(g * group, group)] = rounded[:, lanes]
            cols_x[x, pl.ds(g, 1), :] = sums[:, lanes]
        return 0

    lax.fori_loop(0, nz // 2, pair, 0)

    col_copies = [send(cols_x.at[x], cols_x.at[x], cx_s.at[e], cx_r.at[e], x_dev(e)) for e in x_order]

    lanes_per = chunk // group

    def turn(q):
        at_q = pl.ds(q * chunk, chunk)
        tile_t[:, at_q] = tile[at_q, :].T

    def row_sums(q):
        ones = jnp.ones((16, tile_t.shape[0]), jnp.bfloat16)
        sums = jnp.dot(
            ones, tile_t[:, pl.ds(q * chunk, chunk)], preferred_element_type=jnp.float32
        )
        for i in range(lanes_per):
            rows_all[lm, q * lanes_per + i : q * lanes_per + i + 1, :] = sums[
                0:1, i * group : (i + 1) * group
            ]

    turn(0)
    turn(1)
    for copy in col_copies:
        copy.wait_recv()
    cols_z[z] = jnp.sum(cols_x[...], axis=0)
    col_copies = [send(cols_z.at[z], cols_z.at[z], cz_s.at[d], cz_r.at[d], z_dev(d)) for d in z_order]
    for q in range(2, chunks):
        turn(q)
    for q in range(chunks):
        row_sums(q)
    row_copies = [
        send(rows_all.at[lm], rows_all.at[lm], row_s.at[f], row_r.at[f], lm_dev(f)) for f in lm_order
    ]
    for copy in vec_copies:
        copy.wait_recv()
    for copy in col_copies:
        copy.wait_recv()
    col_scale = lax.rsqrt(jnp.sum(cols_z[...], axis=0) * (1.0 / total_points))
    for g in range(nz):
        scaled[:, g * group : (g + 1) * group] = (vec_z[g] * col_scale[g : g + 1, :]).astype(
            jnp.bfloat16
        )
    col_inv[...] = col_scale

    for q in range(chunks):
        at_q = pl.ds(q * chunk, chunk)
        part[:, at_q] = jnp.dot(
            scaled[...], tile_t[:, at_q], preferred_element_type=jnp.float32
        ).astype(jnp.bfloat16)
        for f in lm_order:
            k = q * nlm + f
            send(
                part.at[:, at(q * chunk + lm_at(f) * piece, piece)], part_in.at[q, lm],
                ps_s.at[k], ps_r.at[k], lm_dev(f),
            )
    for copy in row_copies:
        copy.wait_recv()
    rows_inv[...] = lax.rsqrt(jnp.sum(rows_all[...], axis=0) * (1.0 / total_landmarks))
    for q in range(chunks):
        mine_q = at(q * chunk + lm * piece, piece)
        total = part[:, mine_q].astype(jnp.float32)
        for f in lm_order:
            k = q * nlm + f
            remote(
                part.at[:, pl.ds(0, piece)], part_in.at[q, 0], ps_s.at[k], ps_r.at[k], lm_dev(f)
            ).wait_recv()
        for f in lm_order:
            total = total + part_in[q, lm_at(f)].astype(jnp.float32)
        per = piece // group
        first = q * lanes_per + lm * per
        scale = jnp.concatenate([rows_inv[pl.ds(first + i, 1), :] for i in range(per)], axis=1)
        proj[:, mine_q] = (total * scale * (1.0 / math.sqrt(total_landmarks))).astype(jnp.bfloat16)
        for f in lm_order:
            k = q * nlm + f
            send(proj.at[:, mine_q], proj.at[:, mine_q], pg_s.at[k], pg_r.at[k], lm_dev(f))

    back = jnp.zeros((width, tile.shape[1]), jnp.float32)
    for q in range(chunks):
        at_q = pl.ds(q * chunk, chunk)
        for f in lm_order:
            k = q * nlm + f
            some = proj.at[:, pl.ds(0, piece)]
            remote(some, some, pg_s.at[k], pg_r.at[k], lm_dev(f)).wait_recv()
        values = proj[:, at_q].astype(jnp.float32)
        projected[:, at_q] = values
        scale = jnp.concatenate(
            [rows_inv[q * lanes_per + i : q * lanes_per + i + 1, :] for i in range(lanes_per)], axis=1
        )
        carried = (values * scale).astype(jnp.bfloat16)
        back = back + jnp.dot(carried, tile[at_q, :], preferred_element_type=jnp.float32)

    for g in range(nz):
        back_out[g] = back[:, g * group : (g + 1) * group].astype(jnp.bfloat16)
    copies = [
        send(back_out.at[z_at(d)], back_in.at[z], bz_s.at[d], bz_r.at[d], z_dev(d)) for d in z_order
    ]
    for copy in copies:
        copy.wait_recv()
    total = back_out[z].astype(jnp.float32)
    for d in z_order:
        total = total + back_in[z_at(nz - d)].astype(jnp.float32)
    back_x[x] = total
    copies = [send(back_x.at[x], back_x.at[x], bx_s.at[e], bx_r.at[e], x_dev(e)) for e in x_order]
    for copy in copies:
        copy.wait_recv()
    total = jnp.sum(back_x[...], axis=0) * (
        col_inv[pl.ds(z, 1), :] * (1.0 / math.sqrt(total_points))
    )
    wide = jnp.concatenate([total, jnp.zeros((group - width, group), jnp.float32)], axis=0)
    turned = wide.T
    chosen = turned[:own, :]
    for i in range(1, NX):
        chosen = jnp.where(x == i, turned[i * own : (i + 1) * own, :], chosen)
    new_block[...] = chosen[:, :width]

    for copy in sent:
        copy.wait_send()


def on_device(points, landmarks, block_vec):
    npt, nlm = lax.axis_size("pt"), lax.axis_size("lm")
    count, depth = points.shape
    own, width = block_vec.shape
    nz = npt // NX
    held = npt * own
    group = NX * own
    chunks = 4
    piece = count // chunks // nlm
    f32, bf16 = jnp.float32, jnp.bfloat16
    dma = lambda n: pltpu.SemaphoreType.DMA((n,))
    vmem = pl.BlockSpec(memory_space=pltpu.VMEM)
    new_block, projected = pl.pallas_call(
        functools.partial(kernel, npt, nlm, count * npt, held * nlm),
        out_shape=(
            jax.ShapeDtypeStruct((own, width), f32),
            jax.ShapeDtypeStruct((width, count), f32),
        ),
        in_specs=[pl.BlockSpec(memory_space=pl.ANY), vmem, vmem],
        out_specs=(vmem, vmem),
        scratch_shapes=[
            pltpu.VMEM((count, depth), f32),
            pltpu.VMEM((count, depth), bf16),
            pltpu.VMEM((held, depth), bf16),
            pltpu.VMEM((count, held), bf16),
            pltpu.VMEM((held, count), bf16),
            pltpu.VMEM((NX, nz, group), f32),
            pltpu.VMEM((nz, nz, group), f32),
            pltpu.VMEM((nz, group), f32),
            pltpu.VMEM((NX, width, group), f32),
            pltpu.VMEM((nz, width, group), f32),
            pltpu.VMEM((width, held), bf16),
            pltpu.VMEM((nlm, count // group, group), f32),
            pltpu.VMEM((count // group, group), f32),
            pltpu.VMEM((width, count), bf16),
            pltpu.VMEM((chunks, nlm, width, piece), bf16),
            pltpu.VMEM((width, count), bf16),
            pltpu.VMEM((nz, width, group), bf16),
            pltpu.VMEM((nz, width, group), bf16),
            pltpu.VMEM((NX, width, group), f32),
            dma(8),
            dma(nz), dma(nz),
            dma(npt), dma(npt),
            dma(NX), dma(NX),
            dma(nz), dma(nz),
            dma(NX), dma(NX),
            dma(nz), dma(nz),
            dma(nlm), dma(nlm),
            dma(chunks * nlm), dma(chunks * nlm),
            dma(chunks * nlm), dma(chunks * nlm),
            dma(nz), dma(nz),
            dma(NX), dma(NX),
        ],
        compiler_params=pltpu.CompilerParams(
            collective_id=0, has_side_effects=True, vmem_limit_bytes=60 * 2**20
        ),
    )(points, landmarks, block_vec)
    return new_block, projected.T


def solution(mesh):
    return jax.shard_map(
        on_device,
        mesh=mesh,
        in_specs=(P("pt", None), P(("lm", "pt"), None), P(("lm", "pt"), None)),
        out_specs=(P(("lm", "pt"), None), P("pt", None)),
        check_vma=False,
    )
```

time: 533 us -> 66.5 us (0.12)
  waiting for transfers between devices: 252 us -> 0 us
  blocking collectives: 193 us -> 0 us
  Pallas kernels: 0 us -> 61.7 us
  matrix products: 48.3 us -> 0 us
  other arithmetic: 20.6 us -> 0 us
  between operations: 14.1 us -> 0.64 us
    reduce_scatter x1 -> x0, waiting for transfers between devices: 208 us -> none  [on_device(): lax.psum_scatter(back_part, 'pt', scatter_dimension=0, tiled=True)]
    psum x2 -> x0, blocking collectives: 117 us -> none  [the longest x1 59 us: on_device(): row_sum = lax.psum(row_part, 'lm')]
    all_gather x2 -> x0, blocking collectives: 75.6 us -> none  [the longest x1 41.4 us: on_device(): piece = lax.all_gather(unit_lms, 'pt', axis=0, tiled=True)]
    pallas_call x0 -> x1, Pallas kernels: none -> 61.7 us  [on_device(): pl.pallas_call(functools.partial(kernel, npt, nlm, count * npt, held * nl...]
    dot_general x10 -> x0, matrix products: 48.3 us -> none  [the longest x8 25 us: one(): lax.dot_general(rows, piece, (((1,), (1,)), ((), ())), preferred_element_...]
    psum x1 -> x0, waiting for transfers between devices: 44.2 us -> none  [on_device(): product_sum = lax.psum(product_part, 'lm')]
    reduce_sum x3 -> x0, other arithmetic: 12.6 us -> none  [the longest x1 7.99 us: on_device(): row_part = jnp.sum(tile, axis=1, dtype=jnp.float32)]
    convert_element_type x2 -> x0, other arithmetic: 5.46 us -> none  [normalize(): (rows * lax.rsqrt(jnp.sum(rows * rows, axis=1, keepdims=True) + 1e-06)).a...]
  transfers between devices with their start and end apart: 2 -> 0, of which waited for: 2 -> 0; matrix products, arithmetic and copies ran while one was open for 0% -> 0% of each run, Pallas kernels for 0% -> 0%
where the time goes in v1:
time: 66.5 us; the launch traced here: 66 us
  Pallas kernels  61.7 us (93%)
  local copies, waits for them, and re-layouts  3.59 us (5%)
    pallas_call x1, Pallas kernels, on_device(): pl.pallas_call(functools.partial(kernel, npt, nlm, count * npt, held * nl...  61.7 us
    unnamed x2, local copies, waits for them, and re-layouts  3.59 us

profile of v1, /device:TPU:1, one launch (start us, length us, event | category | flops | bytes accessed | tf_op | source)
XLA Modules:
  0.0 66.0 jit_solution(1176060365321870891)
XLA Ops:
  0.6 61.7 %shard_map.50 = (f32[32,32]{1,0:T(8,128)}, f32[32,8192]{1,0:T(8,128)}) custom-call(f32[8192,256]{1,0:T(8,128)} %points.1, f32[32,256]{1,0:T(8,128)} %landmarks.1, f32[32,32]{1,0:T(8,128)} %vectors.1), custom_call_target="tpu_custom_call" | custom-call | tf_op jit(solution)/shard_map/pallas_call | solution.py:286
  62.4 1.3 %copy.7 = f32[32,32]{1,0:T(8,128)} copy(f32[32,32]{1,0:T(8,128)} %get-tuple-element.8) | data formatting | bytes 8192
  63.7 2.3 %copy.8 = f32[8192,32]{0,1:T(8,128)} copy(f32[8192,32]{0,1:T(8,128)} %bitcast.1) | data formatting | bytes 2097152

commit v2 on v1

v2 whole, which is shorter than its diff:
```python
import functools
import math

import jax
import jax.numpy as jnp
from jax import lax
from jax.experimental import pallas as pl
from jax.experimental.pallas import tpu as pltpu
from jax.sharding import PartitionSpec as P

MESH = pl.DeviceIdType.MESH
NX = 4
PAIR = 256
EXP2_SCALE = 16.0 / math.log(2.0)
LAST = (((1,), (1,)), ((), ()))


def unit_rows(rows):
    return (rows * lax.rsqrt(jnp.sum(rows * rows, axis=1, keepdims=True) + 1e-06)).astype(
        jnp.bfloat16
    )


def at(start, size):
    return pl.ds(pl.multiple_of(start, size), size)


def kernel(
    npt, nlm, total_points, total_landmarks,
    points, landmarks_in, vectors_in, new_block, projected,
    raw, landmarks, vectors, unit, lms, tile, tile_t, cols, col_inv, vec_x, vec_z, scaled, rows_part, rows_got, rows_inv,
    part, part_in, proj, proj_out, back_out, back_in,
    raw_sem, own_sem, out_sem, lz_s, lz_r, lx_s, lx_r, vx_s, vx_r, vz_s, vz_r, c_s, c_r,
    row_s, row_r, ps_s, ps_r, pg_s, pg_r, b_s, b_r,
):
    count, depth = unit.shape
    own, width = vectors.shape
    nz = npt // NX
    group = NX * own
    chunks = part_in.shape[0]
    chunk = count // chunks
    piece = chunk // nlm
    pt = lax.axis_index("pt")
    lm = lax.axis_index("lm")
    z, x = pt // NX, lax.rem(pt, NX)

    def z_at(step):
        return lax.rem(z + step, nz)

    def x_at(step):
        return lax.rem(x + step, NX)

    def lm_at(step):
        return lax.rem(lm + step, nlm)

    def z_dev(step):
        return (z_at(step) * NX + x, lm)

    def x_dev(step):
        return (z * NX + x_at(step), lm)

    def pt_at(step):
        return lax.rem(pt + step, npt)

    def pt_dev(step):
        return (pt_at(step), lm)

    def lm_dev(step):
        return (pt, lm_at(step))

    def remote(src, dst, send, recv, device):
        return pltpu.make_async_remote_copy(
            src_ref=src, dst_ref=dst, send_sem=send, recv_sem=recv,
            device_id=device, device_id_type=MESH,
        )

    sent = []

    def send(*args):
        copy = remote(*args)
        copy.start()
        sent.append(copy)
        return copy

    def drain():
        for copy in sent:
            copy.wait_send()
        sent.clear()

    near, far = [1, nz - 1], [2, nz - 2, 3, nz - 3, 4]
    z_order = far[::-1] + near
    x_order = [1, 3, 2]
    lm_order = list(range(1, nlm))
    pt_order = sorted(range(1, npt), key=lambda step: -min(step, npt - step))

    own_loads = [
        pltpu.make_async_copy(landmarks_in, landmarks, own_sem.at[0]),
        pltpu.make_async_copy(vectors_in, vectors, own_sem.at[1]),
    ]
    for load in own_loads:
        load.start()

    parts = raw_sem.shape[0]
    rows_in = count // parts

    def load(i):
        rows = at(i * rows_in, rows_in)
        return pltpu.make_async_copy(points.at[rows, :], raw.at[rows, :], raw_sem.at[i])

    for i in range(parts):
        load(i).start()

    barrier = pltpu.get_barrier_semaphore()
    for step in pt_order:
        pl.semaphore_signal(barrier, inc=1, device_id=pt_dev(step), device_id_type=MESH)
    for f in lm_order:
        pl.semaphore_signal(barrier, inc=1, device_id=lm_dev(f), device_id_type=MESH)

    own_loads[0].wait()
    lms[at(pt * own, own), :] = unit_rows(landmarks[...])
    pl.semaphore_wait(barrier, len(pt_order) + len(lm_order))

    def lm_rows(zz, xx):
        return lms.at[at((zz * NX + xx) * own, own), :]

    mine = lm_rows(z, x)
    for d in z_order:
        send(mine, mine, lz_s.at[d], lz_r.at[d], z_dev(d))
    for d in [0] + near:
        for e in x_order:
            device = (z_at(d) * NX + x_at(e), lm)
            send(mine, mine, lx_s.at[d * NX + e], lx_r.at[d * NX + e], device)

    own_loads[1].wait()
    lane = lax.broadcasted_iota(jnp.int32, (width, group), 1)
    wide = jnp.concatenate([vectors[...], jnp.zeros((own, group - width), jnp.float32)], axis=1)
    turned = jnp.concatenate([wide] * NX, axis=0).T[:width, :]
    vec_x[x] = jnp.where(lane // own == x, turned, 0.0)

    vec_copies = [send(vec_x.at[x], vec_x.at[x], vx_s.at[e], vx_r.at[e], x_dev(e)) for e in x_order]

    def unit_part(i, _):
        load(i).wait()
        rows = at(i * rows_in, rows_in)
        unit[rows, :] = unit_rows(raw[rows, :])
        return 0

    def go_on(d):
        block = lm_rows(z_at(nz - d), x)
        remote(block, block, lz_s.at[d], lz_r.at[d], z_dev(d)).wait_recv()
        for e in x_order:
            send(block, block, lx_s.at[d * NX + e], lx_r.at[d * NX + e], x_dev(e))

    lax.fori_loop(0, parts - 2, unit_part, 0)
    go_on(2)
    go_on(nz - 2)
    lax.fori_loop(parts - 2, parts, unit_part, 0)
    go_on(3)
    go_on(nz - 3)
    go_on(4)
    for d in near:
        block = lm_rows(z_at(nz - d), x)
        remote(block, block, lz_s.at[d], lz_r.at[d], z_dev(d)).wait_recv()
    for copy in vec_copies:
        copy.wait_recv()
    vec_z[z] = jnp.sum(vec_x[...], axis=0)
    vec_copies = [send(vec_z.at[z], vec_z.at[z], vz_s.at[d], vz_r.at[d], z_dev(d)) for d in z_order]

    def pair(j, _):
        steps = (lax.rem(nz - j, nz), j + 1)
        groups = [z_at(nz - step) for step in steps]
        for step in steps:
            for e in x_order:
                sem = step * NX + e
                remote(mine, mine, lx_s.at[sem], lx_r.at[sem], x_dev(e)).wait_recv()
        weights = jnp.concatenate([lms[at(g * group, group), :] for g in groups], axis=0)
        scores = lax.dot_general(unit[...], weights, LAST, preferred_element_type=jnp.float32)
        values = jnp.exp2(EXP2_SCALE * scores)
        rounded = values.astype(jnp.bfloat16)
        sums = jnp.sum(values, axis=0, keepdims=True)
        for i, g in enumerate(groups):
            lanes = slice(i * group, (i + 1) * group)
            tile[:, at(g * group, group)] = rounded[:, lanes]
            cols[pt, pl.ds(g, 1), :] = sums[:, lanes]
        return 0

    lax.fori_loop(0, nz // 2, pair, 0)

    col_copies = [
        send(cols.at[pt], cols.at[pt], c_s.at[step], c_r.at[step], pt_dev(step)) for step in pt_order
    ]

    lanes_per = chunk // group
    ones = jnp.ones((16, tile.shape[1]), jnp.bfloat16)

    def turn(q, _):
        at_q = at(q * chunk, chunk)
        block = tile[at_q, :]
        tile_t[:, at_q] = block.T
        sums = lax.dot_general(ones, block, LAST, preferred_element_type=jnp.float32)
        for i in range(lanes_per):
            rows_part[pl.ds(q * lanes_per + i, 1), :] = sums[0:1, i * group : (i + 1) * group]
        return 0

    lax.fori_loop(0, chunks, turn, 0)
    row_rows = rows_part.shape[0] // nlm

    def rows_of(owner):
        return at(owner * row_rows, row_rows)

    row_copies = [
        send(rows_part.at[rows_of(lm_at(f)), :], rows_got.at[lm], row_s.at[f], row_r.at[f], lm_dev(f))
        for f in lm_order
    ]
    for copy in vec_copies:
        copy.wait_recv()
    for copy in col_copies:
        copy.wait_recv()
    col_scale = lax.rsqrt(jnp.sum(cols[...], axis=0) * (1.0 / total_points))
    for g in range(nz):
        scaled[:, g * group : (g + 1) * group] = (vec_z[g] * col_scale[g : g + 1, :]).astype(
            jnp.bfloat16
        )
    col_inv[...] = col_scale

    for q in range(chunks):
        at_q = pl.ds(q * chunk, chunk)
        part[:, at_q] = jnp.dot(
            scaled[...], tile_t[:, at_q], preferred_element_type=jnp.float32
        ).astype(jnp.bfloat16)
        for f in lm_order:
            k = q * nlm + f
            send(
                part.at[:, at(q * chunk + lm_at(f) * piece, piece)], part_in.at[q, lm],
                ps_s.at[k], ps_r.at[k], lm_dev(f),
            )
    for copy in row_copies:
        copy.wait_recv()
    total = rows_part[rows_of(lm), :]
    for f in lm_order:
        total = total + rows_got[lm_at(f)]
    rows_inv[rows_of(lm), :] = lax.rsqrt(total * (1.0 / total_landmarks))
    mine_rows = rows_inv.at[rows_of(lm), :]
    row_copies = [
        send(mine_rows, mine_rows, row_s.at[nlm + f], row_r.at[nlm + f], lm_dev(f)) for f in lm_order
    ]
    for q in range(chunks):
        mine_q = at(q * chunk + lm * piece, piece)
        total = part[:, mine_q].astype(jnp.float32)
        for f in lm_order:
            k = q * nlm + f
            remote(
                part.at[:, pl.ds(0, piece)], part_in.at[q, 0], ps_s.at[k], ps_r.at[k], lm_dev(f)
            ).wait_recv()
        for f in lm_order:
            total = total + part_in[q, lm_at(f)].astype(jnp.float32)
        proj[:, mine_q] = total.astype(jnp.bfloat16)
        for f in lm_order:
            k = q * nlm + f
            send(proj.at[:, mine_q], proj.at[:, mine_q], pg_s.at[k], pg_r.at[k], lm_dev(f))

    outs = [
        pltpu.make_async_copy(
            proj_out.at[:, pl.ds(q * chunk, chunk)],
            projected.at[:, pl.ds(q * chunk, chunk)],
            out_sem.at[q],
        )
        for q in range(chunks)
    ]
    for copy in row_copies:
        copy.wait_recv()
    back = jnp.zeros((width, tile.shape[1]), jnp.float32)
    for q in range(chunks):
        at_q = pl.ds(q * chunk, chunk)
        for f in lm_order:
            k = q * nlm + f
            some = proj.at[:, pl.ds(0, piece)]
            remote(some, some, pg_s.at[k], pg_r.at[k], lm_dev(f)).wait_recv()
        scale = jnp.concatenate(
            [rows_inv[q * lanes_per + i : q * lanes_per + i + 1, :] for i in range(lanes_per)], axis=1
        )
        values = proj[:, at_q].astype(jnp.float32) * scale * (1.0 / math.sqrt(total_landmarks))
        proj_out[:, at_q] = values.astype(jnp.bfloat16)
        outs[q].start()
        carried = (values * scale).astype(jnp.bfloat16)
        back = back + jnp.dot(carried, tile[at_q, :], preferred_element_type=jnp.float32)

    bands = width // 8
    lane = lax.broadcasted_iota(jnp.int32, (8, group), 1) // own
    for g in range(nz):
        piece_g = back[:, g * group : (g + 1) * group] * (
            col_inv[g : g + 1, :] * (1.0 / math.sqrt(total_points))
        )
        for i in range(NX):
            packed = jnp.zeros((8, group), jnp.float32)
            for k in range(bands):
                band = piece_g[k * 8 : (k + 1) * 8, :]
                if k != i:
                    band = pltpu.roll(band, (k - i) % bands * own, 1)
                packed = jnp.where(lane == k, band, packed)
            back_out[g * NX + i] = packed
    copies = [
        send(back_out.at[pt_at(step)], back_in.at[pt], b_s.at[step], b_r.at[step], pt_dev(step))
        for step in pt_order
    ]
    back_in[pt] = back_out[pt]
    del sent[-len(copies) :]
    drain()
    for out in outs:
        out.wait()
    for copy in copies:
        copy.wait_recv()
    total = jnp.sum(back_in[...], axis=0)
    bands_in = [total] + [pltpu.roll(total, group - k * own, 1) for k in range(1, bands)]
    square = jnp.concatenate(bands_in + [jnp.zeros((group - width, group), jnp.float32)], axis=0)
    new_block[...] = square.T[:own, :width]
    for copy in copies:
        copy.wait_send()


def widen(block, rounded, new_block, projected, block_in, rounded_in, wide, in_sem, out_sem):
    chunks = out_sem.shape[0]
    chunk = rounded.shape[1] // chunks
    lanes = [pl.ds(q * chunk, chunk) for q in range(chunks)]
    copy_in = [
        pltpu.make_async_copy(rounded.at[:, at_q], rounded_in.at[:, at_q], in_sem.at[q])
        for q, at_q in enumerate(lanes)
    ] + [pltpu.make_async_copy(block, block_in, in_sem.at[chunks])]
    copy_out = [
        pltpu.make_async_copy(wide.at[:, at_q], projected.at[:, at_q], out_sem.at[q])
        for q, at_q in enumerate(lanes)
    ]
    for copy in copy_in:
        copy.start()
    for q, at_q in enumerate(lanes):
        copy_in[q].wait()
        wide[:, at_q] = rounded_in[:, at_q].astype(jnp.float32)
        copy_out[q].start()
    copy_in[chunks].wait()
    new_block[...] = block_in[...]
    for copy in copy_out:
        copy.wait()


def on_device(points, landmarks, block_vec):
    npt, nlm = lax.axis_size("pt"), lax.axis_size("lm")
    count, depth = points.shape
    own, width = block_vec.shape
    nz = npt // NX
    held = npt * own
    group = NX * own
    chunks = 4
    piece = count // chunks // nlm
    f32, bf16 = jnp.float32, jnp.bfloat16
    dma = lambda n: pltpu.SemaphoreType.DMA((n,))
    vmem = pl.BlockSpec(memory_space=pltpu.VMEM)
    block, rounded = pl.pallas_call(
        functools.partial(kernel, npt, nlm, count * npt, held * nlm),
        out_shape=(
            jax.ShapeDtypeStruct((own, width), f32),
            jax.ShapeDtypeStruct((width, count), bf16),
        ),
        in_specs=[pl.BlockSpec(memory_space=pl.ANY)] * 3,
        out_specs=(vmem, pl.BlockSpec(memory_space=pl.ANY)),
        scratch_shapes=[
            pltpu.VMEM((count, depth), f32),
            pltpu.VMEM((own, depth), f32),
            pltpu.VMEM((own, width), f32),
            pltpu.VMEM((count, depth), bf16),
            pltpu.VMEM((held, depth), bf16),
            pltpu.VMEM((count, held), bf16),
            pltpu.VMEM((held, count), bf16),
            pltpu.VMEM((npt, nz, group), f32),
            pltpu.VMEM((nz, group), f32),
            pltpu.VMEM((NX, width, group), f32),
            pltpu.VMEM((nz, width, group), f32),
            pltpu.VMEM((width, held), bf16),
            pltpu.VMEM((count // group, group), f32),
            pltpu.VMEM((nlm, count // group // nlm, group), f32),
            pltpu.VMEM((count // group, group), f32),
            pltpu.VMEM((width, count), bf16),
            pltpu.VMEM((chunks, nlm, width, piece), bf16),
            pltpu.VMEM((width, count), bf16),
            pltpu.VMEM((width, count), bf16),
            pltpu.VMEM((npt, 8, group), f32),
            pltpu.VMEM((npt, 8, group), f32),
            dma(8), dma(2), dma(chunks),
            dma(nz), dma(nz),
            dma(npt), dma(npt),
            dma(NX), dma(NX),
            dma(nz), dma(nz),
            dma(npt), dma(npt),
            dma(2 * nlm), dma(2 * nlm),
            dma(chunks * nlm), dma(chunks * nlm),
            dma(chunks * nlm), dma(chunks * nlm),
            dma(npt), dma(npt),
        ],
        compiler_params=pltpu.CompilerParams(
            collective_id=0, has_side_effects=True, vmem_limit_bytes=60 * 2**20
        ),
    )(points, landmarks, block_vec)
    new_block, projected = pl.pallas_call(
        widen,
        out_shape=(
            jax.ShapeDtypeStruct((own, width), f32),
            jax.ShapeDtypeStruct((width, count), f32),
        ),
        in_specs=[pl.BlockSpec(memory_space=pltpu.HBM)] * 2,
        out_specs=(vmem, pl.BlockSpec(memory_space=pltpu.HBM)),
        scratch_shapes=[
            pltpu.VMEM((own, width), f32),
            pltpu.VMEM((width, count), bf16),
            pltpu.VMEM((width, count), f32),
            dma(chunks + 1),
            dma(chunks),
        ],
        compiler_params=pltpu.CompilerParams(vmem_limit_bytes=60 * 2**20),
    )(block, rounded)
    return new_block, projected.T


def solution(mesh):
    return jax.shard_map(
        on_device,
        mesh=mesh,
        in_specs=(P("pt", None), P(("lm", "pt"), None), P(("lm", "pt"), None)),
        out_specs=(P(("lm", "pt"), None), P("pt", None)),
        check_vma=False,
    )
```

time: 66.5 us -> 63.5 us (0.955)
  local copies, waits for them, and re-layouts: 3.59 us -> 0 us
  Pallas kernels: 61.7 us -> 62.8 us
    unnamed x2 -> x0, local copies, waits for them, and re-layouts: 3.59 us -> none
    pallas_call x0 -> x1, Pallas kernels: none -> 2.57 us  [on_device(): pl.pallas_call(widen, out_shape=(jax.ShapeDtypeStruct((own, width), f32),...]
    pallas_call x1, Pallas kernels: 61.7 us -> 60.2 us  [on_device(): pl.pallas_call(functools.partial(kernel, npt, nlm, count * npt, held * nl...]
where the time goes in v2:
time: 63.5 us; the launch traced here: 63.4 us
  Pallas kernels  62.8 us (99%)
  between operations  0.64 us (1%)
    pallas_call x1, Pallas kernels, on_device(): pl.pallas_call(functools.partial(kernel, npt, nlm, count * npt, held * nl...  60.2 us
    pallas_call x1, Pallas kernels, on_device(): pl.pallas_call(widen, out_shape=(jax.ShapeDtypeStruct((own, width), f32),...  2.57 us

profile of v2, /device:TPU:1, one launch (start us, length us, event | category | flops | bytes accessed | tf_op | source)
XLA Modules:
  0.0 63.4 jit_solution(16027297792131747839)
XLA Ops:
  0.6 60.2 %shard_map.50 = (f32[32,32]{1,0:T(8,128)}, bf16[32,8192]{1,0:T(8,128)(2,1)}) custom-call(f32[8192,256]{1,0:T(8,128)} %points.1, f32[32,256]{1,0:T(8,128)} %landmarks_in.1, f32[32,32]{1,0:T(8,128)} %vectors_in.1), custom_call_target="tpu_custom_call" | custom-call | tf_op jit(solution)/shard_map/pallas_call | solution.py:357
  60.8 2.6 %shard_map.51 = (f32[32,32]{1,0:T(8,128)}, f32[32,8192]{1,0:T(8,128)}) custom-call(f32[32,32]{1,0:T(8,128)} %get-tuple-element.6.block, bf16[32,8192]{1,0:T(8,128)(2,1)} %get-tuple-element.7.rounded), custom_call_target="tpu_custom_call" | custom-call | tf_op jit(solution)/shard_map/pallas_call | solution.py:402
